TPU v7x, 32 devices: a whole 2x2x4 slice. The times are simulated.
32 devices in a mesh: crop: 2 (over y), row: 4 (over z), chan: 2 (over x), sub: 2 (over core).
Axes of the slice: x: 2, y: 2, z: 4, core: 2. Of those that a mesh axis runs over, the one named last changes fastest.
Arguments:
- pair_state: bfloat16 [192, 96, 128], P(('crop', 'row'), ('chan', 'sub')), parts along dimension 0, may hold values from -6 to 6
- chain_lengths: int32 [8], P('crop'), parts along dimension 0, may hold values from 1 to 24, 72 in all
- proj_weights: bfloat16 [2, 128, 640], replicated, may hold values from -0.5 to 0.5
- out_weights: bfloat16 [2, 128, 128], replicated, may hold values from -0.5 to 0.5
- input_gains: float32 [2, 128], replicated, may hold values from 0.25 to 1.75
- output_gains: float32 [2, 128], replicated, may hold values from 0.25 to 1.75
Outputs:
- updated_pair: bfloat16 [192, 96, 128], P(('crop', 'row'), ('chan', 'sub')), parts along dimension 0
There are 2 independent parts, one for each index of `crop`. A program takes and returns all parts, laid end to end along the dimension named above; an argument that names none is the same for every part. Nothing has to cross between parts.
Inputs may be any that keep to these rules, and one draw needn't show every extreme that they name: Chain slot s covers residues s * 24 to (s + 1) * 24 - 1, of which the first chain_lengths[s] are valid; the lengths sum to 72 and one of them equals 24.
All inputs are finite; a program needn't handle non-finite values.
Results may differ from a plain program's by a relative error of at most 0.01.
Values may be sent and summed in bfloat16 or wider, within the bound.
A program may use at most 64 MiB of HBM per device.

v0:
```python
import jax
import jax.numpy as jnp
from jax import lax
from jax.sharding import PartitionSpec as P

epsilon = 1e-05


def layer_norm(values, gains, feature_axis):
    values = values.astype(jnp.float32)
    average = jnp.mean(values, axis=feature_axis, keepdims=True)
    centred = values - average
    variance = jnp.mean(centred * centred, axis=feature_axis, keepdims=True)
    return centred * lax.rsqrt(variance + epsilon) * gains


def valid_rows(chain_lengths, first_pos, how_many, slot_size):
    positions = first_pos + jnp.arange(how_many, dtype=jnp.int32)
    owners = positions // slot_size
    chain_ids = jnp.arange(chain_lengths.shape[0], dtype=jnp.int32)
    limits = jnp.sum(
        jnp.where(owners[:, None] == chain_ids[None, :], chain_lengths[None, :], 0), axis=1
    )
    return (positions % slot_size < limits).astype(jnp.float32)


def send_channels(left_edges, right_edges):
    hidden, rows_here, cols_here = left_edges.shape
    row_groups = lax.axis_size("row")
    col_groups = lax.axis_size(("chan", "sub"))
    share = hidden // (row_groups * col_groups)
    got_left, got_right = (
        lax.all_to_all(
            left_edges.reshape(hidden, rows_here * cols_here),
            ("row", "chan", "sub"),
            split_axis=0,
            concat_axis=0,
            tiled=True,
        ),
        lax.all_to_all(
            right_edges.reshape(hidden, rows_here * cols_here),
            ("row", "chan", "sub"),
            split_axis=0,
            concat_axis=0,
            tiled=True,
        ),
    )

    def arrange(received):
        received = received.reshape(row_groups, col_groups, share, rows_here, cols_here)
        return jnp.transpose(received, (2, 0, 3, 1, 4)).reshape(
            share, row_groups * rows_here, col_groups * cols_here
        )

    return (arrange(got_left), arrange(got_right))


def send_positions(product, rows_here, cols_here):
    share = product.shape[0]
    row_groups = lax.axis_size("row")
    col_groups = lax.axis_size(("chan", "sub"))
    hidden = share * row_groups * col_groups
    ordered = product.reshape(share, row_groups, rows_here, col_groups, cols_here)
    ordered = jnp.transpose(ordered, (1, 3, 0, 2, 4)).reshape(hidden, rows_here * cols_here)
    returned = lax.all_to_all(
        ordered, ("row", "chan", "sub"), split_axis=0, concat_axis=0, tiled=True
    )
    return returned.reshape(hidden, rows_here, cols_here)


def project(normed, weights, first_col, width):
    return jnp.einsum(
        "ijd,de->eij",
        normed,
        weights[:, first_col : first_col + width],
        preferred_element_type=jnp.float32,
    )


def triangle(source, pair_mask, weights_in, weights_out, gains_in, gains_out, incoming):
    hidden = weights_out.shape[0]
    rows_here = source.shape[0]
    cols_here = source.shape[1]
    normed = layer_norm(source, gains_in, 2).astype(jnp.bfloat16)
    mask_here = pair_mask[None]
    left_edges = (
        mask_here
        * jax.nn.sigmoid(project(normed, weights_in, hidden, hidden))
        * project(normed, weights_in, 0, hidden)
    ).astype(jnp.bfloat16)
    right_edges = (
        mask_here
        * jax.nn.sigmoid(project(normed, weights_in, 3 * hidden, hidden))
        * project(normed, weights_in, 2 * hidden, hidden)
    ).astype(jnp.bfloat16)
    spread_left, spread_right = send_channels(left_edges, right_edges)
    if incoming:
        product = jnp.einsum(
            "cki,ckj->cij", spread_left, spread_right, preferred_element_type=jnp.float32
        )
    else:
        product = jnp.einsum(
            "cik,cjk->cij", spread_left, spread_right, preferred_element_type=jnp.float32
        )
    product = product.astype(jnp.bfloat16)
    returned = send_positions(product, rows_here, cols_here)
    gate_value = jax.nn.sigmoid(
        jnp.einsum(
            "ijd,de->ije", normed, weights_in[:, 4 * hidden :], preferred_element_type=jnp.float32
        )
    )
    renormed = layer_norm(returned, gains_out[:, None, None], 0).astype(jnp.bfloat16)
    update = gate_value * jnp.einsum(
        "cij,ce->ije", renormed, weights_out, preferred_element_type=jnp.float32
    )
    return (source.astype(jnp.float32) + update).astype(jnp.bfloat16)


def body(pair_state, chain_lengths, proj_weights, out_weights, input_gains, output_gains):
    rows_here = pair_state.shape[0]
    cols_here = pair_state.shape[1]
    residues = rows_here * lax.axis_size("row")
    slot_size = residues // chain_lengths.shape[0]
    row_valid = valid_rows(chain_lengths, lax.axis_index("row") * rows_here, rows_here, slot_size)
    col_valid = valid_rows(
        chain_lengths, lax.axis_index(("chan", "sub")) * cols_here, cols_here, slot_size
    )
    pair_mask = row_valid[:, None] * col_valid[None, :]
    middle = triangle(
        pair_state,
        pair_mask,
        proj_weights[0],
        out_weights[0],
        input_gains[0],
        output_gains[0],
        False,
    )
    return triangle(
        middle, pair_mask, proj_weights[1], out_weights[1], input_gains[1], output_gains[1], True
    )


def solution(mesh):
    placed = (P(("crop", "row"), ("chan", "sub"), None), P("crop"), P(), P(), P(), P())
    return jax.shard_map(
        body,
        mesh=mesh,
        in_specs=placed,
        out_specs=P(("crop", "row"), ("chan", "sub"), None),
        check_vma=False,
    )
```

profile of v0, /device:TPU:0, one launch (start us, length us, event | category | flops | bytes accessed | tf_op | source)
XLA Modules:
  0.0 94.6 jit_solution(1909056041787837920)
XLA Ops:
  0.0 0.8 slice_bitcast_fusion.22
  0.8 1.1 %convert_reduce_fusion = f32[24,24]{1,0:T(8,128)S(1)} fusion(bf16[24,24,128]{2,1,0:T(8,128)(2,1)} %param.6), kind=kLoop, calls=%fused_computation.57 | loop fusion | flops 146880 | bytes 149760 | tf_op jit(solution)/shard_map/reduce_sum | solution.py:11
  1.9 0.3 fusion.49
  2.2 1.0 %slice_bitcast_fusion = (bf16[128,640]{1,0:T(8,128)(2,1)S(1)}, bf16[128,640]{1,0:T(8,128)(2,1)S(1)}) fusion(bf16[2,128,640]{2,1,0:T(8,128)(2,1)} %param.8), kind=kLoop, calls=%fused_computation.79 | loop fusion | bytes 655360 | tf_op jit(solution)/shard_map/squeeze | solution.py:139
  3.2 0.1 select_reduce_fusion.1
  3.4 0.4 fusion.18
  3.8 0.4 fusion.34
  4.1 0.4 copy.23
  4.6 1.1 %all_to_all.36 = bf16[16,8,576]{2,1,0:T(8,128)(2,1)} reshape(bf16[128,24,24]{2,1,0:T(8,128)(2,1)S(1)} %copy.23) | data formatting | bytes 294912 | tf_op jit(solution)/shard_map/all_to_all | solution.py:33
  5.7 7.4 %all-to-all-start = ((bf16[16,8,576]{2,1,0:T(8,128)(2,1)}), bf16[16,8,576]{2,1,0:T(8,128)(2,1)S(1)}, u32[]{:S(2)}, u32[]{:S(2)}) async-start(bf16[16,8,576]{2,1,0:T(8,128)(2,1)} %all_to_all.36), calls=%async_computation | async-start | bytes 327680 | tf_op jit(solution)/shard_map/all_to_all | solution.py:33
  13.1 0.4 fusion.14
  13.5 0.4 fusion.33
  13.8 0.4 copy.25
  14.3 1.2 %all_to_all.38 = bf16[16,8,576]{2,1,0:T(8,128)(2,1)} reshape(bf16[128,24,24]{2,1,0:T(8,128)(2,1)S(1)} %copy.25) | data formatting | bytes 294912 | tf_op jit(solution)/shard_map/all_to_all | solution.py:40
  15.4 6.1 %all-to-all-done = bf16[16,8,576]{2,1,0:T(8,128)(2,1)S(1)} async-done(((bf16[16,8,576]{2,1,0:T(8,128)(2,1)}), bf16[16,8,576]{2,1,0:T(8,128)(2,1)S(1)}, u32[]{:S(2)}, u32[]{:S(2)}) %all-to-all-start) | async-done | bytes 147488 | tf_op jit(solution)/shard_map/all_to_all | solution.py:33
  21.6 3.5 %all-to-all-start.1 = ((bf16[16,8,576]{2,1,0:T(8,128)(2,1)}), bf16[16,8,576]{2,1,0:T(8,128)(2,1)S(1)}, u32[]{:S(2)}, u32[]{:S(2)}) async-start(bf16[16,8,576]{2,1,0:T(8,128)(2,1)} %all_to_all.38), calls=%async_computation.1 | async-start | bytes 327680 | tf_op jit(solution)/shard_map/all_to_all | solution.py:40
  25.1 0.7 reshape.288
  25.7 0.6 copy.50
  26.4 0.4 reshape.289
  26.8 6.7 %all-to-all-done.1 = bf16[16,8,576]{2,1,0:T(8,128)(2,1)S(1)} async-done(((bf16[16,8,576]{2,1,0:T(8,128)(2,1)}), bf16[16,8,576]{2,1,0:T(8,128)(2,1)S(1)}, u32[]{:S(2)}, u32[]{:S(2)}) %all-to-all-start.1) | async-done | bytes 147488 | tf_op jit(solution)/shard_map/all_to_all | solution.py:40
  33.5 0.7 reshape.290
  34.2 0.6 copy.49
  34.8 0.4 reshape.291
  35.2 0.2 convolution_convert_fusion.1
  35.4 0.3 reshape.292
  35.8 0.1 copy.48
  35.9 1.1 %all_to_all.40 = bf16[16,8,576]{2,1,0:T(8,128)(2,1)} reshape(bf16[4,4,8,24,24]{4,3,2,1,0:T(8,128)(2,1)S(1)} %bitcast.89) | data formatting | bytes 294912 | tf_op jit(solution)/shard_map/all_to_all | solution.py:65
  37.1 3.6 %all-to-all-start.2 = ((bf16[16,8,576]{2,1,0:T(8,128)(2,1)}), bf16[16,8,576]{2,1,0:T(8,128)(2,1)S(1)}, u32[]{:S(2)}, u32[]{:S(2)}) async-start(bf16[16,8,576]{2,1,0:T(8,128)(2,1)} %all_to_all.40), calls=%async_computation.2 | async-start | bytes 327680 | tf_op jit(solution)/shard_map/all_to_all | solution.py:65
  40.8 0.4 fusion.21
  41.2 7.9 %all-to-all-done.2 = bf16[16,8,576]{2,1,0:T(8,128)(2,1)S(1)} async-done(((bf16[16,8,576]{2,1,0:T(8,128)(2,1)}), bf16[16,8,576]{2,1,0:T(8,128)(2,1)S(1)}, u32[]{:S(2)}, u32[]{:S(2)}) %all-to-all-start.2) | async-done | bytes 147488 | tf_op jit(solution)/shard_map/all_to_all | solution.py:65
  49.3 0.1 fusion.48
  49.4 0.7 convert_element_type.113
  50.0 0.2 copy-done.1
  50.2 0.5 fusion.63
  50.7 0.3 multiply_reduce_fusion
  51.0 0.2 multiply_convert_fusion
  51.2 0.3 fusion.7
  51.5 0.2 fusion.32
  51.7 0.4 copy.29
  52.1 1.1 %all_to_all.42 = bf16[16,8,576]{2,1,0:T(8,128)(2,1)} reshape(bf16[128,24,24]{2,1,0:T(8,128)(2,1)S(1)} %copy.29) | data formatting | bytes 294912 | tf_op jit(solution)/shard_map/all_to_all | solution.py:33
  53.3 3.7 %all-to-all-start.3 = ((bf16[16,8,576]{2,1,0:T(8,128)(2,1)}), bf16[16,8,576]{2,1,0:T(8,128)(2,1)S(1)}, u32[]{:S(2)}, u32[]{:S(2)}) async-start(bf16[16,8,576]{2,1,0:T(8,128)(2,1)} %all_to_all.42), calls=%async_computation.3 | async-start | bytes 327680 | tf_op jit(solution)/shard_map/all_to_all | solution.py:33
  57.0 0.3 fusion.3
  57.3 0.2 fusion.31
  57.5 0.4 copy.31
  57.9 1.1 %all_to_all.44 = bf16[16,8,576]{2,1,0:T(8,128)(2,1)} reshape(bf16[128,24,24]{2,1,0:T(8,128)(2,1)S(1)} %copy.31) | data formatting | bytes 294912 | tf_op jit(solution)/shard_map/all_to_all | solution.py:40
  59.1 6.2 %all-to-all-done.3 = bf16[16,8,576]{2,1,0:T(8,128)(2,1)S(1)} async-done(((bf16[16,8,576]{2,1,0:T(8,128)(2,1)}), bf16[16,8,576]{2,1,0:T(8,128)(2,1)S(1)}, u32[]{:S(2)}, u32[]{:S(2)}) %all-to-all-start.3) | async-done | bytes 147488 | tf_op jit(solution)/shard_map/all_to_all | solution.py:33
  65.2 3.5 %all-to-all-start.4 = ((bf16[16,8,576]{2,1,0:T(8,128)(2,1)}), bf16[16,8,576]{2,1,0:T(8,128)(2,1)S(1)}, u32[]{:S(2)}, u32[]{:S(2)}) async-start(bf16[16,8,576]{2,1,0:T(8,128)(2,1)} %all_to_all.44), calls=%async_computation.4 | async-start | bytes 327680 | tf_op jit(solution)/shard_map/all_to_all | solution.py:40
  68.8 0.7 reshape.293
  69.4 0.6 copy.30
  70.0 0.4 reshape.294
  70.4 6.8 %all-to-all-done.4 = bf16[16,8,576]{2,1,0:T(8,128)(2,1)S(1)} async-done(((bf16[16,8,576]{2,1,0:T(8,128)(2,1)}), bf16[16,8,576]{2,1,0:T(8,128)(2,1)S(1)}, u32[]{:S(2)}, u32[]{:S(2)}) %all-to-all-start.4) | async-done | bytes 147488 | tf_op jit(solution)/shard_map/all_to_all | solution.py:40
  77.2 0.7 reshape.295
  77.9 0.6 copy.47
  78.5 0.4 reshape.296
  78.9 0.2 convolution_convert_fusion
  79.1 0.3 reshape.297
  79.4 0.1 copy.46
  79.5 1.1 %all_to_all.46 = bf16[16,8,576]{2,1,0:T(8,128)(2,1)} reshape(bf16[4,4,8,24,24]{4,3,2,1,0:T(8,128)(2,1)S(1)} %bitcast.92) | data formatting | bytes 294912 | tf_op jit(solution)/shard_map/all_to_all | solution.py:65
  80.7 3.5 %all-to-all-start.5 = ((bf16[16,8,576]{2,1,0:T(8,128)(2,1)}), bf16[16,8,576]{2,1,0:T(8,128)(2,1)S(1)}, u32[]{:S(2)}, u32[]{:S(2)}) async-start(bf16[16,8,576]{2,1,0:T(8,128)(2,1)} %all_to_all.46), calls=%async_computation.5 | async-start | bytes 327680 | tf_op jit(solution)/shard_map/all_to_all | solution.py:65
  84.3 0.3 fusion.10
  84.6 8.1 %all-to-all-done.5 = bf16[16,8,576]{2,1,0:T(8,128)(2,1)S(1)} async-done(((bf16[16,8,576]{2,1,0:T(8,128)(2,1)}), bf16[16,8,576]{2,1,0:T(8,128)(2,1)S(1)}, u32[]{:S(2)}, u32[]{:S(2)}) %all-to-all-start.5) | async-done | bytes 147488 | tf_op jit(solution)/shard_map/all_to_all | solution.py:65
  92.8 0.1 fusion.45
  92.9 0.7 convert_element_type.122
  93.5 1.0 %fusion.28 = bf16[24,24,128]{2,1,0:T(8,128)(2,1)} fusion(f32[24,24,128]{2,1,0:T(8,128)S(1)} %get-tuple-element.14, f32[24,24,128]{2,1,0:T(8,128)S(1)} %fusion.10, bf16[128,24,24]{2,1,0:T(8,128)(2,1)S(1)} %convert_element_type.122, bf16[2,128,128]{2,1,0:T(8,128)(2,1)S(1)} %copy-done.1), kind=kOutput, calls=%fused_computation.42 | convolution fusion | flops 19095552 | bytes 1556480 | tf_op jit(solution)/shard_map/cij,ce->ije/dot_general | solution.py:113
  (26 shorter events, 0.6 us)
Async XLA Ops:
  0.0 1.9 %copy-start = (bf16[24,24,128]{2,1,0:T(8,128)(2,1)S(1)}, bf16[24,24,128]{2,1,0:T(8,128)(2,1)}, u32[]{:S(2)}) copy-start(bf16[24,24,128]{2,1,0:T(8,128)(2,1)} %param.6) | copy-start | bytes 442372
  2.2 1.0 %copy-start.3 = (s32[4]{0:T(128)S(1)}, s32[4]{0:T(128)}, u32[]{:S(2)}) copy-start(s32[4]{0:T(128)} %param.7) | copy-start | bytes 52
  5.7 15.8 %all-to-all-start = ((bf16[16,8,576]{2,1,0:T(8,128)(2,1)}), bf16[16,8,576]{2,1,0:T(8,128)(2,1)S(1)}, u32[]{:S(2)}, u32[]{:S(2)}) async-start(bf16[16,8,576]{2,1,0:T(8,128)(2,1)} %all_to_all.36), calls=%async_computation | async-start | bytes 327680 | tf_op jit(solution)/shard_map/all_to_all | solution.py:33
  21.6 11.9 %all-to-all-start.1 = ((bf16[16,8,576]{2,1,0:T(8,128)(2,1)}), bf16[16,8,576]{2,1,0:T(8,128)(2,1)S(1)}, u32[]{:S(2)}, u32[]{:S(2)}) async-start(bf16[16,8,576]{2,1,0:T(8,128)(2,1)} %all_to_all.38), calls=%async_computation.1 | async-start | bytes 327680 | tf_op jit(solution)/shard_map/all_to_all | solution.py:40
  37.1 3.7 %copy-start.2 = (f32[2,128]{1,0:T(2,128)S(1)}, f32[2,128]{1,0:T(2,128)}, u32[]{:S(2)}) copy-start(f32[2,128]{1,0:T(2,128)} %param.11) | copy-start | bytes 3076
  37.1 12.1 %all-to-all-start.2 = ((bf16[16,8,576]{2,1,0:T(8,128)(2,1)}), bf16[16,8,576]{2,1,0:T(8,128)(2,1)S(1)}, u32[]{:S(2)}, u32[]{:S(2)}) async-start(bf16[16,8,576]{2,1,0:T(8,128)(2,1)} %all_to_all.40), calls=%async_computation.2 | async-start | bytes 327680 | tf_op jit(solution)/shard_map/all_to_all | solution.py:65
  49.4 0.8 copy-start.1
  53.3 11.9 %all-to-all-start.3 = ((bf16[16,8,576]{2,1,0:T(8,128)(2,1)}), bf16[16,8,576]{2,1,0:T(8,128)(2,1)S(1)}, u32[]{:S(2)}, u32[]{:S(2)}) async-start(bf16[16,8,576]{2,1,0:T(8,128)(2,1)} %all_to_all.42), calls=%async_computation.3 | async-start | bytes 327680 | tf_op jit(solution)/shard_map/all_to_all | solution.py:33
  65.2 11.9 %all-to-all-start.4 = ((bf16[16,8,576]{2,1,0:T(8,128)(2,1)}), bf16[16,8,576]{2,1,0:T(8,128)(2,1)S(1)}, u32[]{:S(2)}, u32[]{:S(2)}) async-start(bf16[16,8,576]{2,1,0:T(8,128)(2,1)} %all_to_all.44), calls=%async_computation.4 | async-start | bytes 327680 | tf_op jit(solution)/shard_map/all_to_all | solution.py:40
  80.7 11.9 %all-to-all-start.5 = ((bf16[16,8,576]{2,1,0:T(8,128)(2,1)}), bf16[16,8,576]{2,1,0:T(8,128)(2,1)S(1)}, u32[]{:S(2)}, u32[]{:S(2)}) async-start(bf16[16,8,576]{2,1,0:T(8,128)(2,1)} %all_to_all.46), calls=%async_computation.5 | async-start | bytes 327680 | tf_op jit(solution)/shard_map/all_to_all | solution.py:65
where the time goes:
time: 95.3 us; the launch traced here: 94.6 us
  waiting for transfers between devices  41.8 us (44%)
  starting transfers between devices  25.3 us (27%)
  local copies, waits for them, and re-layouts  19.6 us (21%)
  matrix products  5.03 us (5%)
  other arithmetic  2.44 us (3%)
    all_to_all x2, waiting for transfers between devices, send_positions(): lax.all_to_all(ordered, ('row', 'chan', 'sub'), split_axis=0, concat_axis...  16 us
    all_to_all x2, waiting for transfers between devices, send_channels(): lax.all_to_all(right_edges.reshape(hidden, rows_here * cols_here), ('row'...  13.5 us
    all_to_all x2, waiting for transfers between devices, send_channels(): lax.all_to_all(left_edges.reshape(hidden, rows_here * cols_here), ('row',...  12.3 us
    all_to_all x2, starting transfers between devices, send_channels(): lax.all_to_all(left_edges.reshape(hidden, rows_here * cols_here), ('row',...  11.1 us
    all_to_all x2, starting transfers between devices, send_positions(): lax.all_to_all(ordered, ('row', 'chan', 'sub'), split_axis=0, concat_axis...  7.16 us
    all_to_all x2, starting transfers between devices, send_channels(): lax.all_to_all(right_edges.reshape(hidden, rows_here * cols_here), ('row'...  7.03 us
    reshape x8, local copies, waits for them, and re-layouts, arrange(): received.reshape(row_groups, col_groups, share, rows_here, cols_here)  5.03 us
    dot_general x8, matrix products, project(): jnp.einsum('ijd,de->eij', normed, weights[:, first_col:first_col + width]...  2.43 us
  transfers between devices with their start and end apart: 6, of which 6 were waited for; matrix products, arithmetic and copies ran while one was open for 7% of the time, Pallas kernels for 0%

commit v1 on v0

v1 whole, which is shorter than its diff:
```python
import functools

import jax
import jax.numpy as jnp
from jax import lax
from jax.experimental import pallas as pl
from jax.experimental.pallas import tpu as pltpu
from jax.sharding import PartitionSpec as P

MESH = pl.DeviceIdType.MESH
epsilon = 1e-05
f32 = jnp.float32
bf16 = jnp.bfloat16


def layer_norm(values, gains):
    average = jnp.mean(values, axis=-1, keepdims=True)
    centred = values - average
    variance = jnp.mean(centred * centred, axis=-1, keepdims=True)
    return centred * lax.rsqrt(variance + epsilon) * gains


def valid_at(lengths_ref, positions, slot):
    valid = jnp.zeros(positions.shape, f32)
    for chain in range(lengths_ref.shape[0]):
        first = chain * slot
        inside = (positions >= first) & (positions < first + lengths_ref[chain])
        valid = jnp.where(inside, 1.0, valid)
    return valid


def partial_product(left_ref, right, depth, store):
    count = left_ref.shape[1]

    def block(b, carry):
        first = pl.multiple_of(b * 8, 8)

        def step(k, sums):
            other = right(k)
            return tuple(
                total + left_ref[k, pl.ds(first + n, 1), :] * other
                for n, total in enumerate(sums)
            )

        zero = jnp.zeros(right(0).shape, f32)
        sums = lax.fori_loop(0, depth, step, (zero,) * 8, unroll=8)
        for n, total in enumerate(sums):
            store(first + n, total)
        return carry

    lax.fori_loop(0, count // 8, block, 0)


def kernel(
    rows_n, chans, subs, slot,
    x_ref, lengths_ref, w_ref, wo_ref, gi_ref, go_ref, out_ref,
    left, right, gate, mid, total,
    r_send, r_recv, p_send, p_recv, l_send, l_recv, q_send, q_recv,
    r_ssem, r_rsem, p_ssem, p_rsem, l_ssem, l_rsem, q_ssem, q_rsem,
):
    rows, cols, feat = x_ref.shape
    cols_n = chans * subs
    per_col = cols // rows
    row = lax.axis_index("row")
    chan, sub = lax.axis_index("chan"), lax.axis_index("sub")
    col = chan * subs + sub

    def in_row(other):
        return {"chan": other // subs, "sub": lax.rem(other, subs)}

    barrier = pltpu.get_barrier_semaphore()
    for t in range(1, rows_n):
        pl.semaphore_signal(
            barrier, inc=1, device_id={"row": lax.rem(row + t, rows_n)}, device_id_type=MESH
        )
    for t in range(1, cols_n):
        pl.semaphore_signal(
            barrier, inc=1, device_id=in_row(lax.rem(col + t, cols_n)), device_id_type=MESH
        )

    def positions(start, shape, axis):
        return start + lax.broadcasted_iota(jnp.int32, shape, axis)

    row_lead = valid_at(lengths_ref, positions(row * rows, (rows, 1, feat), 0), slot)
    col_lead = valid_at(lengths_ref, positions(col * cols, (cols, 1, feat), 0), slot)
    row_line = valid_at(lengths_ref, positions(row * rows, (1, rows, feat), 1), slot)
    col_line = valid_at(lengths_ref, positions(col * cols, (1, cols, feat), 1), slot)

    def edges(normed, mask, module, first):
        both = jnp.dot(
            normed, w_ref[module, :, first : first + 2 * feat], preferred_element_type=f32
        )
        return mask * jax.nn.sigmoid(both[:, feat:]) * both[:, :feat]

    def flat(values):
        return values.reshape(values.shape[0] * values.shape[1], values.shape[2])

    def copy(source, target, send, receive, device):
        return pltpu.make_async_remote_copy(
            src_ref=source, dst_ref=target, send_sem=send, recv_sem=receive,
            device_id=device, device_id_type=MESH,
        )

    source = flat(x_ref[...].astype(f32))
    normed = layer_norm(source, gi_ref[0:1, :])
    turned = flat(jnp.swapaxes(normed.reshape(rows, cols, feat), 0, 1)).astype(bf16)
    mask = flat(col_lead * row_line)
    right_now = edges(turned, mask, 0, 2 * feat).astype(bf16)
    r_send[...] = right_now
    pl.semaphore_wait(barrier, rows_n + cols_n - 2)

    def r_copy(t):
        other = lax.rem(row + t, rows_n)
        return copy(r_send, r_recv.at[row], r_ssem.at[other], r_rsem.at[row], {"row": other})

    for t in range(1, rows_n):
        r_copy(t).start()
    right[: cols, : rows, :] = right_now.astype(f32).reshape(cols, rows, feat)
    left[: cols, : rows, :] = (
        edges(turned, mask, 0, 0).astype(bf16).astype(f32).reshape(cols, rows, feat)
    )
    gate[...] = jax.nn.sigmoid(
        jnp.dot(normed.astype(bf16), w_ref[0, :, 4 * feat :], preferred_element_type=f32)
    )

    def p_copy(other):
        owner, place = other // per_col, lax.rem(other, per_col)
        return copy(
            p_send.at[other], p_recv.at[col, place], p_ssem.at[other],
            p_rsem.at[col, place], in_row(owner),
        )

    for t in range(rows_n):
        other = lax.rem(row + t, rows_n)
        if t > 0:
            copy(
                r_send, r_recv.at[other], r_ssem.at[other], r_rsem.at[other], {"row": other}
            ).wait_recv()
            right[: cols, : rows, :] = r_recv[other].astype(f32).reshape(cols, rows, feat)

        def store(i, value):
            total[pl.ds(pl.multiple_of(i * rows, 8), rows), :] = value

        partial_product(
            left.at[: cols, : rows, :], lambda k: right[k, : rows, :], cols, store
        )
        owner, place = other // per_col, lax.rem(other, per_col)
        p_send[other] = total[: rows * rows, :].astype(bf16)

        @pl.when(owner != col)
        def _():
            p_copy(other).start()

        @pl.when(owner == col)
        def _():
            p_recv[col, place] = p_send[other]

    pieces = []
    for place in range(per_col):
        pieces.append(p_recv[col, place].astype(f32))
    for t in range(1, cols_n):
        other = lax.rem(col + t, cols_n)
        for place in range(per_col):
            copy(
                p_send.at[0], p_recv.at[other, place], p_ssem.at[0],
                p_rsem.at[other, place], in_row(other),
            ).wait_recv()
            pieces[place] += p_recv[other, place].astype(f32)
    product = jnp.concatenate(
        [piece.reshape(rows, rows, feat) for piece in pieces], axis=1
    )
    product = flat(product)

    def finish(product, source, module):
        renormed = layer_norm(product, go_ref[module : module + 1, :]).astype(bf16)
        update = gate[...] * jnp.dot(renormed, wo_ref[module], preferred_element_type=f32)
        return (source + update).astype(bf16)

    middle = finish(product, flat(x_ref[...].astype(f32)), 0).astype(f32)
    mid[...] = middle

    normed = layer_norm(middle, gi_ref[1:2, :]).astype(bf16)
    mask = flat(row_lead * col_line)
    left_now = edges(normed, mask, 1, 0).astype(bf16)
    l_send[...] = left_now

    def l_copy(t):
        other = lax.rem(col + t, cols_n)
        return copy(l_send, l_recv.at[col], l_ssem.at[other], l_rsem.at[col], in_row(other))

    for t in range(1, cols_n):
        l_copy(t).start()
    left[: rows, : cols, :] = left_now.astype(f32).reshape(rows, cols, feat)
    right[: rows, : cols, :] = (
        edges(normed, mask, 1, 2 * feat).astype(bf16).astype(f32).reshape(rows, cols, feat)
    )

    def q_copy(block):
        return copy(
            q_send.at[block], q_recv.at[row], q_ssem.at[block], q_rsem.at[row], {"row": block}
        )

    for t in range(cols_n):
        other = lax.rem(col + t, cols_n)
        if t > 0:
            copy(
                l_send, l_recv.at[other], l_ssem.at[other], l_rsem.at[other], in_row(other)
            ).wait_recv()
            left[: rows, : cols, :] = l_recv[other].astype(f32).reshape(rows, cols, feat)

        def store(i, value):
            total[pl.ds(pl.multiple_of(i * cols, 8), cols), :] = value

        partial_product(
            left.at[: rows, : cols, :], lambda k: right[k, : cols, :], rows, store
        )
        for place in range(per_col):
            block = other * per_col + place
            size = rows * cols
            q_send[block] = total[place * size : (place + 1) * size, :].astype(bf16)

            @pl.when(block != row)
            def _():
                q_copy(block).start()

            @pl.when(block == row)
            def _():
                q_recv[row] = q_send[block]

        if t == 0:
            gate[...] = jax.nn.sigmoid(
                jnp.dot(normed, w_ref[1, :, 4 * feat :], preferred_element_type=f32)
            )

    product = q_recv[row].astype(f32)
    for t in range(1, rows_n):
        other = lax.rem(row + t, rows_n)
        copy(
            q_send.at[0], q_recv.at[other], q_ssem.at[0], q_rsem.at[other], {"row": other}
        ).wait_recv()
        product += q_recv[other].astype(f32)
    out_ref[...] = finish(product, mid[...], 1).astype(f32).reshape(rows, cols, feat).astype(bf16)

    for t in range(1, rows_n):
        r_copy(t).wait_send()
    for t in range(1, cols_n):
        l_copy(t).wait_send()
    for other in range(rows_n):

        @pl.when(other // per_col != col)
        def _():
            p_copy(other).wait_send()

        @pl.when(other != row)
        def _():
            q_copy(other).wait_send()


def solution(mesh):
    rows_n, chans, subs = mesh.shape["row"], mesh.shape["chan"], mesh.shape["sub"]
    cols_n = chans * subs

    def body(pair_state, chain_lengths, proj_weights, out_weights, input_gains, output_gains):
        rows, cols, feat = pair_state.shape
        slot = rows * rows_n // chain_lengths.shape[0]
        per_col = cols // rows
        pairs = rows * cols
        vmem = pl.BlockSpec(memory_space=pltpu.VMEM)
        dma = pltpu.SemaphoreType.DMA
        return pl.pallas_call(
            functools.partial(kernel, rows_n, chans, subs, slot),
            out_shape=jax.ShapeDtypeStruct(pair_state.shape, bf16),
            in_specs=[vmem, pl.BlockSpec(memory_space=pltpu.SMEM)] + [vmem] * 4,
            out_specs=vmem,
            scratch_shapes=[
                pltpu.VMEM((cols, cols, feat), f32),
                pltpu.VMEM((cols, cols, feat), f32),
                pltpu.VMEM((pairs, feat), f32),
                pltpu.VMEM((pairs, feat), f32),
                pltpu.VMEM((cols * cols, feat), f32),
                pltpu.VMEM((pairs, feat), bf16),
                pltpu.VMEM((rows_n, pairs, feat), bf16),
                pltpu.VMEM((rows_n, rows * rows, feat), bf16),
                pltpu.VMEM((cols_n, per_col, rows * rows, feat), bf16),
                pltpu.VMEM((pairs, feat), bf16),
                pltpu.VMEM((cols_n, pairs, feat), bf16),
                pltpu.VMEM((rows_n, pairs, feat), bf16),
                pltpu.VMEM((rows_n, pairs, feat), bf16),
                dma((rows_n,)), dma((rows_n,)),
                dma((rows_n,)), dma((cols_n, per_col)),
                dma((cols_n,)), dma((cols_n,)),
                dma((rows_n,)), dma((rows_n,)),
            ],
            compiler_params=pltpu.CompilerParams(
                collective_id=0, has_side_effects=True, vmem_limit_bytes=48 * 1024 * 1024
            ),
        )(pair_state, chain_lengths, proj_weights, out_weights, input_gains, output_gains)

    placed = (P(("crop", "row"), ("chan", "sub"), None), P("crop"), P(), P(), P(), P())
    return jax.shard_map(
        body,
        mesh=mesh,
        in_specs=placed,
        out_specs=P(("crop", "row"), ("chan", "sub"), None),
        check_vma=False,
    )
```

time: 95.3 us -> 48.8 us (0.51)
  the two profiles are of different devices: /device:TPU:0 before, /device:TPU:25 now
where the time goes in v1:
time: 48.8 us; the launch traced here: 48.6 us
  Pallas kernels  43.1 us (88%)
  local copies, waits for them, and re-layouts  5.4 us (11%)
    pallas_call x1, Pallas kernels, body(): pl.pallas_call(functools.partial(kernel, rows_n, chans, subs, slot), out_...  43.1 us
    unnamed x13, local copies, waits for them, and re-layouts  5.4 us

profile of v1, /device:TPU:25, one launch (start us, length us, event | category | flops | bytes accessed | tf_op | source)
XLA Modules:
  0.0 48.6 jit_solution(16443701817708597846)
XLA Ops:
  0.0 0.0 copy-start
  0.0 1.0 %copy-done = bf16[2,128,640]{2,1,0:T(8,128)(2,1)S(1)} copy-done((bf16[2,128,640]{2,1,0:T(8,128)(2,1)S(1)}, bf16[2,128,640]{2,1,0:T(8,128)(2,1)}, u32[]{:S(2)}) %copy-start) | copy-done | bytes 327704
  1.0 0.0 copy-start.1
  1.0 0.9 %copy-done.1 = bf16[24,24,128]{2,1,0:T(8,128)(2,1)S(1)} copy-done((bf16[24,24,128]{2,1,0:T(8,128)(2,1)S(1)}, bf16[24,24,128]{2,1,0:T(8,128)(2,1)}, u32[]{:S(2)}) %copy-start.1) | copy-done | bytes 147480
  1.9 0.0 copy-start.2
  1.9 0.8 %copy-done.2 = bf16[2,128,128]{2,1,0:T(8,128)(2,1)S(1)} copy-done((bf16[2,128,128]{2,1,0:T(8,128)(2,1)S(1)}, bf16[2,128,128]{2,1,0:T(8,128)(2,1)}, u32[]{:S(2)}) %copy-start.2) | copy-done | bytes 65560
  2.7 0.0 copy-start.3
  2.7 0.7 %copy-done.3 = f32[2,128]{1,0:T(2,128)S(1)} copy-done((f32[2,128]{1,0:T(2,128)S(1)}, f32[2,128]{1,0:T(2,128)}, u32[]{:S(2)}) %copy-start.3) | copy-done | bytes 1048
  3.4 0.0 copy-start.4
  3.4 0.7 %copy-done.4 = f32[2,128]{1,0:T(2,128)S(1)} copy-done((f32[2,128]{1,0:T(2,128)S(1)}, f32[2,128]{1,0:T(2,128)}, u32[]{:S(2)}) %copy-start.4) | copy-done | bytes 1048
  4.1 0.0 copy-start.5
  4.1 0.7 %copy-done.5 = s32[4]{0:T(128)S(1)} copy-done((s32[4]{0:T(128)S(1)}, s32[4]{0:T(128)}, u32[]{:S(2)}) %copy-start.5) | copy-done | bytes 40
  4.7 43.1 %shard_map.64 = bf16[24,24,128]{2,1,0:T(8,128)(2,1)S(1)} custom-call(bf16[24,24,128]{2,1,0:T(8,128)(2,1)S(1)} %copy-done.1, s32[4]{0:T(128)S(1)} %copy-done.5, bf16[2,128,640]{2,1,0:T(8,128)(2,1)S(1)} %copy-done, bf16[2,128,128]{2,1,0:T(8,128)(2,1)S(1)} %copy-done.2, f32[2,128]{1,0:T(2,128)S(1)} %copy-done.3, f32[2,128]{1,0:T(2,128)S(1)} %copy-done.4), custom_call_target="tpu_custom_call" | custom-call | tf_op jit(solution)/shard_map/pallas_call | solution.py:270
  47.9 0.7 %copy.8 = bf16[24,24,128]{2,1,0:T(8,128)(2,1)} copy(bf16[24,24,128]{2,1,0:T(8,128)(2,1)S(1)} %shard_map.64) | data formatting | bytes 294912
Async XLA Ops:
  0.0 1.0 %copy-start = (bf16[2,128,640]{2,1,0:T(8,128)(2,1)S(1)}, bf16[2,128,640]{2,1,0:T(8,128)(2,1)}, u32[]{:S(2)}) copy-start(bf16[2,128,640]{2,1,0:T(8,128)(2,1)} %w_ref.1) | copy-start | bytes 983044
  1.0 0.9 %copy-start.1 = (bf16[24,24,128]{2,1,0:T(8,128)(2,1)S(1)}, bf16[24,24,128]{2,1,0:T(8,128)(2,1)}, u32[]{:S(2)}) copy-start(bf16[24,24,128]{2,1,0:T(8,128)(2,1)} %x_ref.1) | copy-start | bytes 442372
  1.9 0.8 %copy-start.2 = (bf16[2,128,128]{2,1,0:T(8,128)(2,1)S(1)}, bf16[2,128,128]{2,1,0:T(8,128)(2,1)}, u32[]{:S(2)}) copy-start(bf16[2,128,128]{2,1,0:T(8,128)(2,1)} %wo_ref.1) | copy-start | bytes 196612
  2.7 0.7 %copy-start.3 = (f32[2,128]{1,0:T(2,128)S(1)}, f32[2,128]{1,0:T(2,128)}, u32[]{:S(2)}) copy-start(f32[2,128]{1,0:T(2,128)} %gi_ref.1) | copy-start | bytes 3076
  3.4 0.7 %copy-start.4 = (f32[2,128]{1,0:T(2,128)S(1)}, f32[2,128]{1,0:T(2,128)}, u32[]{:S(2)}) copy-start(f32[2,128]{1,0:T(2,128)} %go_ref.1) | copy-start | bytes 3076
  4.1 0.7 %copy-start.5 = (s32[4]{0:T(128)S(1)}, s32[4]{0:T(128)}, u32[]{:S(2)}) copy-start(s32[4]{0:T(128)} %lengths_ref.1) | copy-start | bytes 52

commit v2 on v1

--- a/solution.py
+++ b/solution.py
@@ -53,11 +53,23 @@
 
 def kernel(
     rows_n, chans, subs, slot,
-    x_ref, lengths_ref, w_ref, wo_ref, gi_ref, go_ref, out_ref,
+    x_hbm, lengths_hbm, w_hbm, wo_hbm, gi_hbm, go_hbm, out_ref,
+    x_ref, lengths_ref, w_ref, wo_ref, gi_ref, go_ref, load_sem,
     left, right, gate, mid, total,
     r_send, r_recv, p_send, p_recv, l_send, l_recv, q_send, q_recv,
     r_ssem, r_rsem, p_ssem, p_rsem, l_ssem, l_rsem, q_ssem, q_rsem,
 ):
+    loads = [
+        pltpu.make_async_copy(source, target, load_sem.at[n])
+        for n, (source, target) in enumerate(
+            [
+                (x_hbm, x_ref), (gi_hbm, gi_ref), (lengths_hbm, lengths_ref),
+                (w_hbm, w_ref), (go_hbm, go_ref), (wo_hbm, wo_ref),
+            ]
+        )
+    ]
+    for load in loads:
+        load.start()
     rows, cols, feat = x_ref.shape
     cols_n = chans * subs
     per_col = cols // rows
@@ -78,6 +90,8 @@
             barrier, inc=1, device_id=in_row(lax.rem(col + t, cols_n)), device_id_type=MESH
         )
 
+    loads[2].wait()
+
     def positions(start, shape, axis):
         return start + lax.broadcasted_iota(jnp.int32, shape, axis)
 
@@ -101,10 +115,13 @@
             device_id=device, device_id_type=MESH,
         )
 
+    loads[0].wait()
+    loads[1].wait()
     source = flat(x_ref[...].astype(f32))
     normed = layer_norm(source, gi_ref[0:1, :])
     turned = flat(jnp.swapaxes(normed.reshape(rows, cols, feat), 0, 1)).astype(bf16)
     mask = flat(col_lead * row_line)
+    loads[3].wait()
     right_now = edges(turned, mask, 0, 2 * feat).astype(bf16)
     r_send[...] = right_now
     pl.semaphore_wait(barrier, rows_n + cols_n - 2)
@@ -155,6 +172,8 @@
         def _():
             p_recv[col, place] = p_send[other]
 
+    loads[4].wait()
+    loads[5].wait()
     pieces = []
     for place in range(per_col):
         pieces.append(p_recv[col, place].astype(f32))
@@ -270,9 +289,16 @@
         return pl.pallas_call(
             functools.partial(kernel, rows_n, chans, subs, slot),
             out_shape=jax.ShapeDtypeStruct(pair_state.shape, bf16),
-            in_specs=[vmem, pl.BlockSpec(memory_space=pltpu.SMEM)] + [vmem] * 4,
+            in_specs=[pl.BlockSpec(memory_space=pl.ANY)] * 6,
             out_specs=vmem,
             scratch_shapes=[
+                pltpu.VMEM(pair_state.shape, bf16),
+                pltpu.SMEM(chain_lengths.shape, jnp.int32),
+                pltpu.VMEM(proj_weights.shape, bf16),
+                pltpu.VMEM(out_weights.shape, bf16),
+                pltpu.VMEM(input_gains.shape, f32),
+                pltpu.VMEM(output_gains.shape, f32),
+                dma((6,)),
                 pltpu.VMEM((cols, cols, feat), f32),
                 pltpu.VMEM((cols, cols, feat), f32),
                 pltpu.VMEM((pairs, feat), f32),
@@ -292,7 +318,7 @@
                 dma((rows_n,)), dma((rows_n,)),
             ],
             compiler_params=pltpu.CompilerParams(
-                collective_id=0, has_side_effects=True, vmem_limit_bytes=48 * 1024 * 1024
+                collective_id=0, has_side_effects=True, vmem_limit_bytes=60 * 1024 * 1024
             ),
         )(pair_state, chain_lengths, proj_weights, out_weights, input_gains, output_gains)
 

time: 48.8 us -> 45 us (0.922)
  the two profiles are of different devices: /device:TPU:25 before, /device:TPU:11 now
where the time goes in v2:
time: 45 us; the launch traced here: 44.8 us
  Pallas kernels  43.2 us (96%)
  local copies, waits for them, and re-layouts  1.59 us (4%)
    pallas_call x1, Pallas kernels, body(): pl.pallas_call(functools.partial(kernel, rows_n, chans, subs, slot), out_...  43.2 us
    unnamed x1, local copies, waits for them, and re-layouts  1.59 us

profile of v2, /device:TPU:11, one launch (start us, length us, event | category | flops | bytes accessed | tf_op | source)
XLA Modules:
  0.0 44.8 jit_solution(11251346051418046841)
XLA Ops:
  0.0 43.2 %shard_map.64 = bf16[24,24,128]{2,1,0:T(8,128)(2,1)} custom-call(bf16[24,24,128]{2,1,0:T(8,128)(2,1)} %x_hbm.1, s32[4]{0:T(128)} %lengths_hbm.1, bf16[2,128,640]{2,1,0:T(8,128)(2,1)} %w_hbm.1, bf16[2,128,128]{2,1,0:T(8,128)(2,1)} %wo_hbm.1, f32[2,128]{1,0:T(2,128)} %gi_hbm.1, f32[2,128]{1,0:T(2,128)} %go_hbm.1), custom_call_target="tpu_custom_call" | custom-call | tf_op jit(solution)/shard_map/pallas_call | solution.py:289
  43.2 1.6 %copy.8 = bf16[24,24,128]{2,1,0:T(8,128)(2,1)} copy(bf16[24,24,128]{2,1,0:T(8,128)(2,1)} %shard_map.64) | data formatting | bytes 294912

commit v3 on v2

v3 whole, which is shorter than its diff:
```python
import functools

import jax
import jax.numpy as jnp
from jax import lax
from jax.experimental import pallas as pl
from jax.experimental.pallas import tpu as pltpu
from jax.sharding import PartitionSpec as P

MESH = pl.DeviceIdType.MESH
epsilon = 1e-05
f32 = jnp.float32
bf16 = jnp.bfloat16


def layer_norm(values, gains):
    average = jnp.mean(values, axis=-1, keepdims=True)
    centred = values - average
    variance = jnp.mean(centred * centred, axis=-1, keepdims=True)
    return centred * lax.rsqrt(variance + epsilon) * gains


def valid_at(lengths_ref, positions, slot):
    valid = jnp.zeros(positions.shape, f32)
    for chain in range(lengths_ref.shape[0]):
        first = chain * slot
        inside = (positions >= first) & (positions < first + lengths_ref[chain])
        valid = jnp.where(inside, 1.0, valid)
    return valid


def partial_product(left, right, depth, count, store):
    def step(k, sums):
        other = right(k)
        return tuple(total + left(k, i) * other for i, total in enumerate(sums))

    zero = jnp.zeros(right(0).shape, f32)
    sums = lax.fori_loop(0, depth, step, (zero,) * count, unroll=8)
    for i, total in enumerate(sums):
        store(i, total)


def kernel(
    rows_n, chans, subs, slot,
    x_hbm, lengths_hbm, w_hbm, wo_hbm, gi_hbm, go_hbm, out_ref,
    x_ref, lengths_ref, w_ref, wo_ref, gi_ref, go_ref, load_sem,
    left, right, part, gate, mid, total,
    r_send, r_recv, p_send, p_recv, p_own, l_send, l_recv, q_send, q_recv,
    r_ssem, r_rsem, p_ssem, p_rsem, l_ssem, l_rsem, q_ssem, q_rsem,
):
    loads = [
        pltpu.make_async_copy(source, target, load_sem.at[n])
        for n, (source, target) in enumerate(
            [
                (x_hbm, x_ref), (gi_hbm, gi_ref), (lengths_hbm, lengths_ref),
                (w_hbm, w_ref), (go_hbm, go_ref), (wo_hbm, wo_ref),
            ]
        )
    ]
    for load in loads:
        load.start()
    rows, cols, feat = x_ref.shape
    cols_n = chans * subs
    per_col = cols // rows
    chunks = rows // 8
    row = lax.axis_index("row")
    chan, sub = lax.axis_index("chan"), lax.axis_index("sub")
    col = chan * subs + sub

    def in_row(other):
        return {"chan": other // subs, "sub": lax.rem(other, subs)}

    up, down = lax.rem(row + 1, rows_n), lax.rem(row + rows_n - 1, rows_n)
    barrier = pltpu.get_barrier_semaphore()
    pl.semaphore_signal(barrier, inc=1, device_id={"row": down}, device_id_type=MESH)
    for t in range(1, cols_n):
        pl.semaphore_signal(
            barrier, inc=1, device_id=in_row(lax.rem(col + t, cols_n)), device_id_type=MESH
        )

    loads[2].wait()

    def positions(start, shape, axis):
        return start + lax.broadcasted_iota(jnp.int32, shape, axis)

    row_lead = valid_at(lengths_ref, positions(row * rows, (rows, 1, feat), 0), slot)
    col_lead = valid_at(lengths_ref, positions(col * cols, (cols, 1, feat), 0), slot)
    row_line = valid_at(lengths_ref, positions(row * rows, (1, rows, feat), 1), slot)
    col_line = valid_at(lengths_ref, positions(col * cols, (1, cols, feat), 1), slot)

    def edges(normed, mask, module, first):
        both = jnp.dot(
            normed, w_ref[module, :, first : first + 2 * feat], preferred_element_type=f32
        )
        return mask * jax.nn.sigmoid(both[:, feat:]) * both[:, :feat]

    def flat(values):
        return values.reshape(values.shape[0] * values.shape[1], values.shape[2])

    def copy(source, target, send, receive, device):
        return pltpu.make_async_remote_copy(
            src_ref=source, dst_ref=target, send_sem=send, recv_sem=receive,
            device_id=device, device_id_type=MESH,
        )

    loads[0].wait()
    loads[1].wait()
    source = flat(x_ref[...].astype(f32))
    normed = layer_norm(source, gi_ref[0:1, :])
    turned = flat(jnp.swapaxes(normed.reshape(rows, cols, feat), 0, 1)).astype(bf16)
    mask = flat(col_lead * row_line)
    loads[3].wait()
    right_now = edges(turned, mask, 0, 2 * feat).reshape(cols, rows, feat)
    for c in range(chunks):
        r_send[c] = flat(right_now[:, 8 * c : 8 * c + 8, :]).astype(bf16)
    pl.semaphore_wait(barrier, cols_n)

    def r_copy(origin, c, held):
        return copy(held, r_recv.at[origin, c], r_ssem.at[origin, c], r_rsem.at[origin, c], {"row": up})

    def p_copy(origin, c):
        owner, place = origin // per_col, lax.rem(origin, per_col)
        return copy(
            p_send.at[origin, c], p_recv.at[col, place, c], p_ssem.at[origin, c],
            p_rsem.at[col, place, c], in_row(owner),
        )

    def spread(origin, c, held):
        part[: cols, :, :] = held[...].astype(f32).reshape(cols, 8, feat)

        def store(i, value):
            total[8 * i : 8 * i + 8, :] = value

        partial_product(
            lambda k, i: left[k, i : i + 1, :], lambda k: part[k], cols, rows, store
        )
        owner, place = origin // per_col, lax.rem(origin, per_col)

        @pl.when(owner != col)
        def _():
            p_send[origin, c] = total[: 8 * rows, :].astype(bf16)
            p_copy(origin, c).start()

        @pl.when(owner == col)
        def _():
            p_own[place, c] = total[: 8 * rows, :]

    for c in range(chunks):
        r_copy(row, c, r_send.at[c]).start()
    left[: cols, : rows, :] = (
        edges(turned, mask, 0, 0).astype(bf16).astype(f32).reshape(cols, rows, feat)
    )
    gate[...] = jax.nn.sigmoid(
        jnp.dot(normed.astype(bf16), w_ref[0, :, 4 * feat :], preferred_element_type=f32)
    )
    for c in range(chunks):
        spread(row, c, r_send.at[c])

    def r_step(s, carry):
        origin = lax.rem(row + rows_n - s, rows_n)
        for c in range(chunks):
            held = r_recv.at[origin, c]
            r_copy(origin, c, held).wait_recv()

            @pl.when(s < rows_n - 1)
            def _():
                r_copy(origin, c, held).start()

            spread(origin, c, held)
        return carry

    lax.fori_loop(1, rows_n, r_step, 0)

    loads[4].wait()
    loads[5].wait()
    pieces = []
    for place in range(per_col):
        for c in range(chunks):
            piece = p_own[place, c]
            for t in range(1, cols_n):
                other = lax.rem(col + t, cols_n)
                copy(
                    p_send.at[0, c], p_recv.at[other, place, c], p_ssem.at[0, c],
                    p_rsem.at[other, place, c], in_row(other),
                ).wait_recv()
                piece += p_recv[other, place, c].astype(f32)
            pieces.append(piece.reshape(rows, 8, feat))
    product = flat(jnp.concatenate(pieces, axis=1))

    def finish(product, source, module):
        renormed = layer_norm(product, go_ref[module : module + 1, :]).astype(bf16)
        update = gate[...] * jnp.dot(renormed, wo_ref[module], preferred_element_type=f32)
        return (source + update).astype(bf16)

    middle = finish(product, flat(x_ref[...].astype(f32)), 0).astype(f32)
    mid[...] = middle

    normed = layer_norm(middle, gi_ref[1:2, :]).astype(bf16)
    mask = flat(row_lead * col_line)
    left_now = edges(normed, mask, 1, 0).reshape(rows, cols, feat)
    for place in range(per_col):
        for c in range(chunks):
            first = place * rows + 8 * c
            l_send[place, c] = flat(left_now[:, first : first + 8, :]).astype(bf16)

    def dest(s):
        return lax.rem(row + 2 * rows_n - 1 - s, rows_n)

    def l_copy(d, c, other):
        place = lax.rem(d, per_col)
        return copy(
            l_send.at[place, c], l_recv.at[d, c], l_ssem.at[place, c, other],
            l_rsem.at[d, c], in_row(other),
        )

    def l_start(d):
        @pl.when(d // per_col == col)
        def _():
            for c in range(chunks):
                for t in range(1, cols_n):
                    l_copy(d, c, lax.rem(col + t, cols_n)).start()

    def q_copy(d, c):
        return copy(
            q_send.at[d, c], q_recv.at[d, c], q_ssem.at[d, c], q_rsem.at[d, c], {"row": up}
        )

    l_start(dest(0))
    right[: rows, : cols, :] = (
        edges(normed, mask, 1, 2 * feat).astype(bf16).astype(f32).reshape(rows, cols, feat)
    )
    gate[...] = jax.nn.sigmoid(
        jnp.dot(normed, w_ref[1, :, 4 * feat :], preferred_element_type=f32)
    )

    def q_step(s, first_step, last_step):
        d = dest(s)
        size = 8 * cols
        for c in range(chunks):
            @pl.when(d // per_col != col)
            def _():
                l_copy(d, c, col).wait_recv()
                part[: rows, :, :] = l_recv[d, c].astype(f32).reshape(rows, 8, feat)

            @pl.when(d // per_col == col)
            def _():
                part[: rows, :, :] = (
                    l_send[lax.rem(d, per_col), c].astype(f32).reshape(rows, 8, feat)
                )

            if c == 0 and not last_step:
                l_start(dest(s + 1))

            def store(i, value):
                total[c * size + i * cols : c * size + (i + 1) * cols, :] = value

            partial_product(
                lambda k, i: part[k, i : i + 1, :], lambda k: right[k, : cols, :], rows, 8, store
            )
            here = slice(c * size, (c + 1) * size)
            if not first_step:
                q_copy(d, c).wait_recv()
            if not last_step:
                value = total[here, :]
                if not first_step:
                    value += q_recv[d, c].astype(f32)
                q_send[d, c] = value.astype(bf16)
                q_copy(d, c).start()
            else:
                total[here, :] += q_recv[d, c].astype(f32)

    q_step(0, True, False)

    def q_between(s, carry):
        q_step(s, False, False)
        return carry

    lax.fori_loop(1, rows_n - 1, q_between, 0)
    q_step(rows_n - 1, False, True)
    product = total[: rows * cols, :]
    out_ref[...] = finish(product, mid[...], 1).astype(f32).reshape(rows, cols, feat).astype(bf16)

    for c in range(chunks):
        for s in range(rows_n - 1):
            origin = lax.rem(row + rows_n - s, rows_n)
            r_copy(origin, c, r_send.at[c]).wait_send()
            q_copy(dest(s), c).wait_send()
        for place in range(per_col):
            for t in range(1, cols_n):
                l_copy(place, c, lax.rem(col + t, cols_n)).wait_send()
        for origin in range(rows_n):

            @pl.when(origin // per_col != col)
            def _():
                p_copy(origin, c).wait_send()


def solution(mesh):
    rows_n, chans, subs = mesh.shape["row"], mesh.shape["chan"], mesh.shape["sub"]
    cols_n = chans * subs

    def body(pair_state, chain_lengths, proj_weights, out_weights, input_gains, output_gains):
        rows, cols, feat = pair_state.shape
        slot = rows * rows_n // chain_lengths.shape[0]
        per_col = cols // rows
        pairs, chunks = rows * cols, rows // 8
        vmem = pl.BlockSpec(memory_space=pltpu.VMEM)
        dma = pltpu.SemaphoreType.DMA
        return pl.pallas_call(
            functools.partial(kernel, rows_n, chans, subs, slot),
            out_shape=jax.ShapeDtypeStruct(pair_state.shape, bf16),
            in_specs=[pl.BlockSpec(memory_space=pl.ANY)] * 6,
            out_specs=vmem,
            scratch_shapes=[
                pltpu.VMEM(pair_state.shape, bf16),
                pltpu.SMEM(chain_lengths.shape, jnp.int32),
                pltpu.VMEM(proj_weights.shape, bf16),
                pltpu.VMEM(out_weights.shape, bf16),
                pltpu.VMEM(input_gains.shape, f32),
                pltpu.VMEM(output_gains.shape, f32),
                dma((6,)),
                pltpu.VMEM((cols, cols, feat), f32),
                pltpu.VMEM((cols, cols, feat), f32),
                pltpu.VMEM((cols, 8, feat), f32),
                pltpu.VMEM((pairs, feat), f32),
                pltpu.VMEM((pairs, feat), f32),
                pltpu.VMEM((pairs, feat), f32),
                pltpu.VMEM((chunks, cols * 8, feat), bf16),
                pltpu.VMEM((rows_n, chunks, cols * 8, feat), bf16),
                pltpu.VMEM((rows_n, chunks, rows * 8, feat), bf16),
                pltpu.VMEM((cols_n, per_col, chunks, rows * 8, feat), bf16),
                pltpu.VMEM((per_col, chunks, rows * 8, feat), f32),
                pltpu.VMEM((per_col, chunks, rows * 8, feat), bf16),
                pltpu.VMEM((rows_n, chunks, rows * 8, feat), bf16),
                pltpu.VMEM((rows_n, chunks, cols * 8, feat), bf16),
                pltpu.VMEM((rows_n, chunks, cols * 8, feat), bf16),
                dma((rows_n, chunks)), dma((rows_n, chunks)),
                dma((rows_n, chunks)), dma((cols_n, per_col, chunks)),
                dma((per_col, chunks, cols_n)), dma((rows_n, chunks)),
                dma((rows_n, chunks)), dma((rows_n, chunks)),
            ],
            compiler_params=pltpu.CompilerParams(
                collective_id=0, has_side_effects=True, vmem_limit_bytes=60 * 1024 * 1024
            ),
        )(pair_state, chain_lengths, proj_weights, out_weights, input_gains, output_gains)

    placed = (P(("crop", "row"), ("chan", "sub"), None), P("crop"), P(), P(), P(), P())
    return jax.shard_map(
        body,
        mesh=mesh,
        in_specs=placed,
        out_specs=P(("crop", "row"), ("chan", "sub"), None),
        check_vma=False,
    )
```

time: 45 us -> 37 us (0.82)
  the two profiles are of different devices: /device:TPU:11 before, /device:TPU:0 now
where the time goes in v3:
time: 37 us; the launch traced here: 36.9 us
  Pallas kernels  35.3 us (95%)
  local copies, waits for them, and re-layouts  1.59 us (4%)
    pallas_call x1, Pallas kernels, body(): pl.pallas_call(functools.partial(kernel, rows_n, chans, subs, slot), out_...  35.3 us
    unnamed x1, local copies, waits for them, and re-layouts  1.59 us

profile of v3, /device:TPU:0, one launch (start us, length us, event | category | flops | bytes accessed | tf_op | source)
XLA Modules:
  0.0 36.9 jit_solution(3207915938272200768)
XLA Ops:
  0.0 35.3 %shard_map.64 = bf16[24,24,128]{2,1,0:T(8,128)(2,1)} custom-call(bf16[24,24,128]{2,1,0:T(8,128)(2,1)} %x_hbm.1, s32[4]{0:T(128)} %lengths_hbm.1, bf16[2,128,640]{2,1,0:T(8,128)(2,1)} %w_hbm.1, bf16[2,128,128]{2,1,0:T(8,128)(2,1)} %wo_hbm.1, f32[2,128]{1,0:T(2,128)} %gi_hbm.1, f32[2,128]{1,0:T(2,128)} %go_hbm.1), custom_call_target="tpu_custom_call" | custom-call | tf_op jit(solution)/shard_map/pallas_call | solution.py:309
  35.3 1.6 %copy.8 = bf16[24,24,128]{2,1,0:T(8,128)(2,1)} copy(bf16[24,24,128]{2,1,0:T(8,128)(2,1)} %shard_map.64) | data formatting | bytes 294912

commit v4 on v3

--- a/solution.py
+++ b/solution.py
@@ -44,7 +44,7 @@
     rows_n, chans, subs, slot,
     x_hbm, lengths_hbm, w_hbm, wo_hbm, gi_hbm, go_hbm, out_ref,
     x_ref, lengths_ref, w_ref, wo_ref, gi_ref, go_ref, load_sem,
-    left, right, part, gate, mid, total,
+    left, right, part, gate, mid, turned_ref, normed_ref, total,
     r_send, r_recv, p_send, p_recv, p_own, l_send, l_recv, q_send, q_recv,
     r_ssem, r_rsem, p_ssem, p_rsem, l_ssem, l_rsem, q_ssem, q_rsem,
 ):
@@ -103,17 +103,15 @@
             device_id=device, device_id_type=MESH,
         )
 
-    loads[0].wait()
-    loads[1].wait()
-    source = flat(x_ref[...].astype(f32))
-    normed = layer_norm(source, gi_ref[0:1, :])
-    turned = flat(jnp.swapaxes(normed.reshape(rows, cols, feat), 0, 1)).astype(bf16)
-    mask = flat(col_lead * row_line)
-    loads[3].wait()
-    right_now = edges(turned, mask, 0, 2 * feat).reshape(cols, rows, feat)
-    for c in range(chunks):
-        r_send[c] = flat(right_now[:, 8 * c : 8 * c + 8, :]).astype(bf16)
-    pl.semaphore_wait(barrier, cols_n)
+    def set_gate(module):
+        gate[...] = jax.nn.sigmoid(
+            jnp.dot(normed_ref[...], w_ref[module, :, 4 * feat :], preferred_element_type=f32)
+        ).reshape(rows, cols, feat)
+
+    def finish(product, source, gates, module):
+        renormed = layer_norm(product, go_ref[module : module + 1, :]).astype(bf16)
+        update = gates * jnp.dot(renormed, wo_ref[module], preferred_element_type=f32)
+        return (source + update).astype(bf16)
 
     def r_copy(origin, c, held):
         return copy(held, r_recv.at[origin, c], r_ssem.at[origin, c], r_rsem.at[origin, c], {"row": up})
@@ -145,16 +143,28 @@
         def _():
             p_own[place, c] = total[: 8 * rows, :]
 
+    loads[0].wait()
+    loads[1].wait()
+    turned = []
     for c in range(chunks):
+        source = x_ref[8 * c : 8 * c + 8, :, :].astype(f32)
+        normed = layer_norm(source, gi_ref[0:1, :])
+        normed_ref[8 * cols * c : 8 * cols * (c + 1), :] = flat(normed).astype(bf16)
+        turned.append(flat(jnp.swapaxes(normed, 0, 1)).astype(bf16))
+        if c == 0:
+            loads[3].wait()
+        mask = flat(col_lead * row_line[:, 8 * c : 8 * c + 8, :])
+        r_send[c] = edges(turned[c], mask, 0, 2 * feat).astype(bf16)
+        if c == 0:
+            pl.semaphore_wait(barrier, cols_n)
         r_copy(row, c, r_send.at[c]).start()
-    left[: cols, : rows, :] = (
-        edges(turned, mask, 0, 0).astype(bf16).astype(f32).reshape(cols, rows, feat)
-    )
-    gate[...] = jax.nn.sigmoid(
-        jnp.dot(normed.astype(bf16), w_ref[0, :, 4 * feat :], preferred_element_type=f32)
-    )
+    for c in range(chunks):
+        mask = flat(col_lead * row_line[:, 8 * c : 8 * c + 8, :])
+        values = edges(turned[c], mask, 0, 0).astype(bf16).astype(f32)
+        left[: cols, 8 * c : 8 * c + 8, :] = values.reshape(cols, 8, feat)
     for c in range(chunks):
         spread(row, c, r_send.at[c])
+    set_gate(0)
 
     def r_step(s, carry):
         origin = lax.rem(row + rows_n - s, rows_n)
@@ -173,7 +183,28 @@
 
     loads[4].wait()
     loads[5].wait()
-    pieces = []
+    def dest(s):
+        return lax.rem(row + 2 * rows_n - 1 - s, rows_n)
+
+    def l_copy(d, c, other):
+        place = lax.rem(d, per_col)
+        return copy(
+            l_send.at[place, c], l_recv.at[d, c], l_ssem.at[place, c, other],
+            l_rsem.at[d, c], in_row(other),
+        )
+
+    def l_start(d):
+        @pl.when(d // per_col == col)
+        def _():
+            for c in range(chunks):
+                for t in range(1, cols_n):
+                    l_copy(d, c, lax.rem(col + t, cols_n)).start()
+
+    def q_copy(d, c):
+        return copy(
+            q_send.at[d, c], q_recv.at[d, c], q_ssem.at[d, c], q_rsem.at[d, c], {"row": up}
+        )
+
     for place in range(per_col):
         for c in range(chunks):
             piece = p_own[place, c]
@@ -184,54 +215,24 @@
                     p_rsem.at[other, place, c], in_row(other),
                 ).wait_recv()
                 piece += p_recv[other, place, c].astype(f32)
-            pieces.append(piece.reshape(rows, 8, feat))
-    product = flat(jnp.concatenate(pieces, axis=1))
-
-    def finish(product, source, module):
-        renormed = layer_norm(product, go_ref[module : module + 1, :]).astype(bf16)
-        update = gate[...] * jnp.dot(renormed, wo_ref[module], preferred_element_type=f32)
-        return (source + update).astype(bf16)
-
-    middle = finish(product, flat(x_ref[...].astype(f32)), 0).astype(f32)
-    mid[...] = middle
-
-    normed = layer_norm(middle, gi_ref[1:2, :]).astype(bf16)
-    mask = flat(row_lead * col_line)
-    left_now = edges(normed, mask, 1, 0).reshape(rows, cols, feat)
-    for place in range(per_col):
-        for c in range(chunks):
             first = place * rows + 8 * c
-            l_send[place, c] = flat(left_now[:, first : first + 8, :]).astype(bf16)
-
-    def dest(s):
-        return lax.rem(row + 2 * rows_n - 1 - s, rows_n)
-
-    def l_copy(d, c, other):
-        place = lax.rem(d, per_col)
-        return copy(
-            l_send.at[place, c], l_recv.at[d, c], l_ssem.at[place, c, other],
-            l_rsem.at[d, c], in_row(other),
-        )
-
-    def l_start(d):
-        @pl.when(d // per_col == col)
-        def _():
-            for c in range(chunks):
+            here = slice(first, first + 8)
+            source = flat(x_ref[:, here, :].astype(f32))
+            middle = finish(piece, source, flat(gate[:, here, :]), 0).astype(f32)
+            mid[:, here, :] = middle.reshape(rows, 8, feat)
+            turned = layer_norm(middle, gi_ref[1:2, :])
+            turned_ref[:, here, :] = turned.reshape(rows, 8, feat)
+            turned = turned.astype(bf16)
+            mask = flat(row_lead * col_line[:, here, :])
+            l_send[place, c] = edges(turned, mask, 1, 0).astype(bf16)
+
+            @pl.when(dest(0) == col * per_col + place)
+            def _():
                 for t in range(1, cols_n):
-                    l_copy(d, c, lax.rem(col + t, cols_n)).start()
-
-    def q_copy(d, c):
-        return copy(
-            q_send.at[d, c], q_recv.at[d, c], q_ssem.at[d, c], q_rsem.at[d, c], {"row": up}
-        )
-
-    l_start(dest(0))
-    right[: rows, : cols, :] = (
-        edges(normed, mask, 1, 2 * feat).astype(bf16).astype(f32).reshape(rows, cols, feat)
-    )
-    gate[...] = jax.nn.sigmoid(
-        jnp.dot(normed, w_ref[1, :, 4 * feat :], preferred_element_type=f32)
-    )
+                    l_copy(dest(0), c, lax.rem(col + t, cols_n)).start()
+
+            values = edges(turned, mask, 1, 2 * feat).astype(bf16).astype(f32)
+            right[: rows, here, :] = values.reshape(rows, 8, feat)
 
     def q_step(s, first_step, last_step):
         d = dest(s)
@@ -267,9 +268,16 @@
                 q_send[d, c] = value.astype(bf16)
                 q_copy(d, c).start()
             else:
-                total[here, :] += q_recv[d, c].astype(f32)
+                lines = slice(8 * c, 8 * c + 8)
+                updated = finish(
+                    total[here, :] + q_recv[d, c].astype(f32),
+                    flat(mid[lines]), flat(gate[lines]), 1,
+                )
+                out_ref[lines] = updated.astype(f32).reshape(8, cols, feat).astype(bf16)
 
     q_step(0, True, False)
+    normed_ref[...] = flat(turned_ref[...]).astype(bf16)
+    set_gate(1)
 
     def q_between(s, carry):
         q_step(s, False, False)
@@ -277,9 +285,6 @@
 
     lax.fori_loop(1, rows_n - 1, q_between, 0)
     q_step(rows_n - 1, False, True)
-    product = total[: rows * cols, :]
-    out_ref[...] = finish(product, mid[...], 1).astype(f32).reshape(rows, cols, feat).astype(bf16)
-
     for c in range(chunks):
         for s in range(rows_n - 1):
             origin = lax.rem(row + rows_n - s, rows_n)
@@ -322,8 +327,10 @@
                 pltpu.VMEM((cols, cols, feat), f32),
                 pltpu.VMEM((cols, cols, feat), f32),
                 pltpu.VMEM((cols, 8, feat), f32),
-                pltpu.VMEM((pairs, feat), f32),
-                pltpu.VMEM((pairs, feat), f32),
+                pltpu.VMEM((rows, cols, feat), f32),
+                pltpu.VMEM((rows, cols, feat), f32),
+                pltpu.VMEM((rows, cols, feat), f32),
+                pltpu.VMEM((pairs, feat), bf16),
                 pltpu.VMEM((pairs, feat), f32),
                 pltpu.VMEM((chunks, cols * 8, feat), bf16),
                 pltpu.VMEM((rows_n, chunks, cols * 8, feat), bf16),

time: 37 us -> 36.6 us (0.989)
  Pallas kernels: 35.3 us -> 34.9 us
where the time goes in v4:
time: 36.6 us; the launch traced here: 36.5 us
  Pallas kernels  34.9 us (95%)
  local copies, waits for them, and re-layouts  1.59 us (4%)
    pallas_call x1, Pallas kernels, body(): pl.pallas_call(functools.partial(kernel, rows_n, chans, subs, slot), out_...  34.9 us
    unnamed x1, local copies, waits for them, and re-layouts  1.59 us

profile of v4, /device:TPU:0, one launch (start us, length us, event | category | flops | bytes accessed | tf_op | source)
XLA Modules:
  0.0 36.5 jit_solution(14136404247515714238)
XLA Ops:
  0.0 34.9 %shard_map.64 = bf16[24,24,128]{2,1,0:T(8,128)(2,1)} custom-call(bf16[24,24,128]{2,1,0:T(8,128)(2,1)} %x_hbm.1, s32[4]{0:T(128)} %lengths_hbm.1, bf16[2,128,640]{2,1,0:T(8,128)(2,1)} %w_hbm.1, bf16[2,128,128]{2,1,0:T(8,128)(2,1)} %wo_hbm.1, f32[2,128]{1,0:T(2,128)} %gi_hbm.1, f32[2,128]{1,0:T(2,128)} %go_hbm.1), custom_call_target="tpu_custom_call" | custom-call | tf_op jit(solution)/shard_map/pallas_call | solution.py:314
  34.9 1.6 %copy.8 = bf16[24,24,128]{2,1,0:T(8,128)(2,1)} copy(bf16[24,24,128]{2,1,0:T(8,128)(2,1)} %shard_map.64) | data formatting | bytes 294912
